TPU v7x, 128 devices: a whole 4x4x4 slice. The times are simulated.
128 devices in a mesh: dp: 16 (over y, x), chan: 4 (over z_lo, core), row: 2 (over z_hi).
Axes of the slice: x: 4, y: 4, z: 4 (z_hi: 2, z_lo: 2; z = z_hi * 2 + z_lo), core: 2. Of those that a mesh axis runs over, the one named last changes fastest.
Arguments:
- images: bfloat16 [16, 128, 320, 128], P('dp', 'row', 'chan'), may hold values from -6 to 6
- kernel: bfloat16 [9, 320, 320], P(None, 'dp', 'chan'), may hold values from -0.109375 to 0.109375
- cotangent: bfloat16 [16, 128, 320, 128], P('dp', 'row', 'chan'), may hold values from -6 to 6
Outputs:
- activated: bfloat16 [16, 128, 320, 128], P('dp', 'row', 'chan')
- input_grad: float32 [16, 128, 320, 128], P('dp', 'row', 'chan')
- kernel_grad: float32 [9, 320, 320], P(None, 'dp', 'chan')
All inputs are finite; a program needn't handle non-finite values.
Results may differ from a plain program's by a relative error of at most 0.0029.
Values may be sent and summed in bfloat16 or wider, within the bound.
A program may use at most 192 MiB of HBM per device.

v0:
```python
import functools
import math

import jax
import jax.numpy as jnp
from jax import lax
from jax.experimental import pallas as pl
from jax.experimental.pallas import tpu as pltpu
from jax.sharding import PartitionSpec as P

MESH = pl.DeviceIdType.MESH
BF16 = jnp.bfloat16
F32 = jnp.float32
ROWS = 4


def round_up(x, m):
    return (x + m - 1) // m * m


def remote(src, dst, send, recv, **where):
    return pltpu.make_async_remote_copy(
        src_ref=src, dst_ref=dst, send_sem=send, recv_sem=recv, device_id=where, device_id_type=MESH
    )


def shift_right(x):
    lane = lax.broadcasted_iota(jnp.int32, x.shape, 1)
    return jnp.where(lane == 0, 0.0, pltpu.roll(x, 1, 1))


def shift_left(x):
    lane = lax.broadcasted_iota(jnp.int32, x.shape, 1)
    return jnp.where(lane == x.shape[1] - 1, 0.0, pltpu.roll(x, x.shape[1] - 1, 1))


def body(
    side, own, share, height, width,
    img, ker, cot,
    act_out, in_own, in_other, kg_out,
    xs, gs, ss, s3, acc, wk, wpk, wraw, em, wf, wb, ab, pf, pb,
    kin, kp, kr, ksum, kr2, kt, kq,
    local, wsend, wrecv, isend, irecv, hsend, hrecv, bsend, brecv,
    ssend, srecv, asend, arecv, alocal, plocal, psend, precv, csend, crecv, ksend, krecv,
):
    rows = height // 2
    chunks = rows // ROWS
    chip = 2 * own
    every = 4 * own
    pad_share = wpk.shape[1]
    lanes = s3.shape[0] // 2

    dp = lax.axis_index("dp")
    chan = lax.axis_index("chan")
    row = lax.axis_index("row")
    l = chan // 2
    c = lax.rem(chan, 2)
    sib = 2 * l + 1 - c
    other = 2 * (1 - l)
    y = dp // side
    x = lax.rem(dp, side)
    first = jnp.where(c == 0, x, y)
    second = jnp.where(c == 0, y, x)
    step_first = jnp.where(c == 0, 1, side)
    step_second = jnp.where(c == 0, side, 1)

    def on_first(k):
        f = lax.rem(first + k, side)
        return f, f * step_first + second * step_second

    def on_second(k):
        s = lax.rem(second + k, side)
        return s, first * step_first + s * step_second

    barrier = pltpu.get_barrier_semaphore()
    count = 0
    for k in range(1, 4):
        pl.semaphore_signal(barrier, inc=1, device_id={"chan": lax.rem(chan + k, 4)}, device_id_type=MESH)
        count += 1
    for g in range(4):
        pl.semaphore_signal(barrier, inc=1, device_id={"row": 1 - row, "chan": g}, device_id_type=MESH)
        count += 1
    for k in range(1, side):
        pl.semaphore_signal(barrier, inc=1, device_id={"dp": on_first(k)[1]}, device_id_type=MESH)
        pl.semaphore_signal(barrier, inc=1, device_id={"dp": on_second(k)[1]}, device_id_type=MESH)
        count += 2

    def mine(ref, first_row, n, g):
        return ref.at[pl.ds(first_row, n), pl.ds(pl.multiple_of(own * g, 16), own)]

    load_k = pltpu.make_async_copy(ker, wk, local.at[0])
    load_k.start()
    load_x = pltpu.make_async_copy(
        img.at[pl.ds((rows - 1) * c, rows + 1)], mine(xs, 1 - c, rows + 1, chan), local.at[1]
    )
    load_x.start()
    load_g = pltpu.make_async_copy(cot.at[pl.ds(rows * c, rows)], mine(gs, 0, rows, c), local.at[2])
    load_g.start()

    wpk[...] = jnp.zeros_like(wpk)
    for core in range(2):
        s3[core * lanes + 3 * own : (core + 1) * lanes, :] = jnp.zeros((lanes - 3 * own, s3.shape[1]), BF16)

    @pl.when(jnp.logical_and(c == 0, row == 0))
    def _():
        xs[0] = jnp.zeros(xs.shape[1:], BF16)
        ss[0] = jnp.zeros(ss.shape[1:], BF16)

    @pl.when(jnp.logical_and(c == 1, row == 1))
    def _():
        xs[rows + 1] = jnp.zeros(xs.shape[1:], BF16)
        ss[rows + 1] = jnp.zeros(ss.shape[1:], BF16)

    acc[...] = jnp.zeros_like(acc)
    load_k.wait()
    for b in range(3):
        for a in range(3):
            wpk[b, a * share : (a + 1) * share, 0:own] = wk[3 * a + b].astype(F32)
    wraw[c, second, first] = wpk[...].astype(BF16)

    pl.semaphore_wait(barrier, count)

    gather = []
    for k in range(1, side):
        spot = wraw.at[c, second, first]
        copy = remote(spot, spot, wsend.at[0, k], wrecv.at[0, k], dp=on_first(k)[1])
        copy.start()
        gather.append(copy)

    pieces = [(rows - ROWS, ROWS + 1), (1, ROWS + 1)]
    pieces += [(ROWS * k + 2, ROWS) for k in range(1, chunks - 2)]
    pieces += [(ROWS * (chunks - 2) + 2, ROWS - 2)]
    sent = []
    for to in range(2):
        copy = remote(
            img.at[pl.ds(rows - to, 1)], mine(xs, (rows + 1) * (1 - to), 1, chan),
            isend.at[to, chunks], irecv.at[c, chunks], chan=other + to,
        )
        copy.start()
        sent.append(copy)
        copy = remote(
            img.at[pl.ds((height - 1) * (1 - row), 1)], mine(xs, (rows + 1) * row, 1, chan),
            hsend.at[to], hrecv.at[chan], row=1 - row, chan=2 * to + row,
        )
        copy.start()
        sent.append(copy)
    copy = remote(
        img.at[pl.ds((rows - 1) * (1 - c), rows + 1)], mine(xs, c, rows + 1, chan),
        bsend.at[0], brecv.at[0], chan=sib,
    )
    copy.start()
    sent.append(copy)
    for s, (start, n) in enumerate(pieces):
        for to in range(2):
            copy = remote(
                img.at[pl.ds(rows * to + start - 1, n)], mine(xs, start, n, chan),
                isend.at[to, s], irecv.at[c, s], chan=other + to,
            )
            copy.start()
            sent.append(copy)
        if s == 0:
            copy = remote(
                cot.at[pl.ds(rows * (1 - c), rows)], mine(gs, 0, rows, c), bsend.at[1], brecv.at[1], chan=sib
            )
            copy.start()
            sent.append(copy)

    spot = lax.broadcasted_iota(jnp.int32, (1, em.shape[1]), 1)
    owner = jnp.zeros_like(spot)
    for k in range(1, side * side):
        owner += (spot >= k * pad_share).astype(jnp.int32)
    within = spot - owner * pad_share
    tap = (within >= share).astype(jnp.int32) + (within >= 2 * share).astype(jnp.int32)
    target = tap * every + owner * share + within - tap * share
    target = jnp.where(within < 3 * share, target, -1)
    em[...] = (lax.broadcasted_iota(jnp.int32, em.shape, 0) == target).astype(F32).astype(BF16)

    for k in range(1, side):
        gather[k - 1].wait()
    for k in range(1, side):
        spot = wraw.at[c, second]
        copy = remote(spot, spot, wsend.at[1, k], wrecv.at[1, k], dp=on_second(k)[1])
        copy.start()
        gather.append(copy)
    for k in range(1, side):
        gather[side - 2 + k].wait()
    copy = remote(wraw.at[c], wraw.at[c], bsend.at[2], brecv.at[2], chan=sib)
    copy.start()
    sent.append(copy)
    remote(wraw.at[c], wraw.at[1 - c], bsend.at[2], brecv.at[2], chan=sib).wait_recv()

    wide = 2 * wraw.shape[-1]
    fold = (
        lax.broadcasted_iota(jnp.int32, (wide, 3 * chip), 0),
        lax.broadcasted_iota(jnp.int32, (wide, 3 * chip), 1),
    )
    half = wide // 2
    core_of = (fold[0] >= half).astype(jnp.int32)
    inside = fold[0] - core_of * half
    for b in range(3):
        blocks = []
        for core in range(2):
            order = [(i, j) if core == 0 else (j, i) for i in range(side) for j in range(side)]
            blocks.append(jnp.concatenate([wraw[core, i, j, b] for i, j in order], axis=0))
        taps = jnp.dot(em[...], jnp.concatenate(blocks, axis=1), preferred_element_type=F32)
        turned = jnp.transpose(taps).astype(BF16)
        for core in range(2):
            wf[b * chip + core * own : b * chip + (core + 1) * own, :] = turned[core * half : core * half + own]
        narrow = taps.astype(BF16)
        total = jnp.zeros((every, 3 * chip), F32)
        for a in range(3):
            goal = (2 - a) * chip + core_of * own + inside
            place = jnp.logical_and(fold[1] == goal, inside < own).astype(F32).astype(BF16)
            total += jnp.dot(narrow[a * every : (a + 1) * every], place, preferred_element_type=F32)
        total = total.astype(BF16)
        for part in range(2):
            base = pl.multiple_of(b * every + chip * jnp.where(l == part, 0, 1), 16)
            wb[pl.ds(base, chip), :] = total[part * chip : (part + 1) * chip]

    load_x.wait()
    load_g.wait()
    for which, ref in ((0, mine(xs, 1 - c, rows + 1, sib)), (1, mine(gs, 0, rows, 1 - c))):
        remote(ref, ref, bsend.at[which], brecv.at[which], chan=sib).wait_recv()
    for of in range(2):
        ref = mine(xs, (rows + 1) * (1 - c), 1, other + of)
        remote(ref, ref, isend.at[of, chunks], irecv.at[of, chunks], chan=other + of).wait_recv()

    @pl.when(c != row)
    def _():
        for g in range(4):
            ref = mine(xs, (rows + 1) * c, 1, g)
            remote(ref, ref, hsend.at[0], hrecv.at[g], row=1 - row, chan=g).wait_recv()

    def await_rows(s, start, n):
        for of in range(2):
            ref = mine(xs, start, n, other + of)
            remote(ref, ref, isend.at[of, s], irecv.at[of, s], chan=other + of).wait_recv()

    place = 2 * row + c

    def down_copy():
        return remote(ss.at[rows], ss.at[0], ssend.at[0], srecv.at[0], row=row + c, chan=sib)

    def up_copy():
        return remote(ss.at[1], ss.at[rows + 1], ssend.at[1], srecv.at[1], row=row - (1 - c), chan=sib)

    def act_copies(k):
        at = pl.ds(k * ROWS, ROWS)
        to = pl.ds(rows * c + k * ROWS, ROWS)
        return (
            pltpu.make_async_copy(ab.at[c, at], act_out.at[to], alocal.at[k]),
            remote(ab.at[1 - c, at], act_out.at[to], asend.at[k], arecv.at[k], chan=sib),
        )

    def grad_copies(k):
        at = pl.ds(k * ROWS, ROWS)
        to = pl.ds(rows * c + k * ROWS, ROWS)
        return (
            pltpu.make_async_copy(pf.at[c, at], in_own.at[to], plocal.at[k]),
            remote(pf.at[1 - c, at], in_own.at[to], psend.at[k], precv.at[k], chan=sib),
            remote(pb.at[0, at], in_other.at[to], csend.at[0, k], crecv.at[c, k], chan=other),
            remote(pb.at[1, at], in_other.at[to], csend.at[1, k], crecv.at[c, k], chan=other + 1),
        )

    def three(ref, start):
        block = ref[pl.ds(start, 3)]
        return block.reshape(3 * ref.shape[1], width)

    def forward(k):
        for pair in range(ROWS // 2):
            q = k * ROWS + 2 * pair
            right = jnp.concatenate([three(xs, q), three(xs, q + 1)], axis=1)
            taps = jnp.dot(wf[...], right, preferred_element_type=F32)
            for u in range(2):
                at = slice(u * width, (u + 1) * width)
                pre = shift_right(taps[0:chip, at]) + taps[chip : 2 * chip, at] + shift_left(taps[2 * chip :, at])
                sigma = 1.0 / (1.0 + jnp.exp(-pre))
                done = (pre * sigma).astype(BF16)
                for core in range(2):
                    ab[core, q + u] = done[core * own : (core + 1) * own]
                slope = gs[q + u].astype(F32) * sigma * (1.0 + pre * (1.0 - sigma))
                slope = slope.astype(BF16)
                ss[q + u + 1] = slope
                wide_slope = slope.astype(F32)
                turned = (shift_left(wide_slope).astype(BF16), slope, shift_right(wide_slope).astype(BF16))
                to = slice((2 * pair + u) * width, (2 * pair + u + 1) * width)
                for core in range(2):
                    for b in range(3):
                        s3[core * lanes + b * own : core * lanes + (b + 1) * own, to] = turned[b][
                            core * own : (core + 1) * own
                        ]
        left = jnp.concatenate([three(xs, k * ROWS + u) for u in range(ROWS)], axis=1)
        term = lax.dot_general(left, s3[...], (((1,), (1,)), ((), ())), preferred_element_type=F32)
        for core in range(2):
            acc[core] += term[:, core * lanes : (core + 1) * lanes]

    def backward(k):
        for pair in range(ROWS // 2):
            q = k * ROWS + 2 * pair
            right = jnp.concatenate([three(ss, q), three(ss, q + 1)], axis=1)
            taps = jnp.dot(wb[...], right, preferred_element_type=F32)
            for u in range(2):
                at = slice(u * width, (u + 1) * width)
                grad = (
                    shift_left(taps[0:every, at])
                    + taps[every : 2 * every, at]
                    + shift_right(taps[2 * every :, at])
                )
                for core in range(2):
                    pf[core, q + u] = grad[core * own : (core + 1) * own]
                    pb[core, q + u] = grad[chip + core * own : chip + (core + 1) * own].astype(BF16)

    @pl.loop(0, chunks + 3)
    def _(s):
        for fixed in (0, 1, chunks - 1):

            @pl.when(s == fixed)
            def _():
                await_rows(fixed, *pieces[fixed])

        @pl.when(jnp.logical_and(s > 1, s < chunks - 1))
        def _():
            await_rows(s, ROWS * (s - 1) + 2, ROWS)

        @pl.when(s < chunks)
        def _():
            k = lax.rem(s + chunks - 1, chunks)
            forward(k)
            for copy in act_copies(k):
                copy.start()

        @pl.when(jnp.logical_and(s == 0, place < 3))
        def _():
            down_copy().start()

        @pl.when(jnp.logical_and(s == 1, place > 0))
        def _():
            up_copy().start()

        @pl.when(jnp.logical_and(s == chunks + 1, place < 3))
        def _():
            up_copy().wait_recv()

        @pl.when(jnp.logical_and(s == chunks + 2, place > 0))
        def _():
            down_copy().wait_recv()

        @pl.when(s >= 3)
        def _():
            k = lax.rem(s - 2, chunks)
            backward(k)
            for copy in grad_copies(k):
                copy.start()

        @pl.when(s == chunks - 1)
        def _():
            remote(acc.at[1 - c], kin, ksend.at[0, 0], krecv.at[0, 0], chan=sib).start()

    trade = remote(acc.at[1 - c], kin, ksend.at[0, 0], krecv.at[0, 0], chan=sib)
    trade.wait()
    kin[...] += acc[c]
    for i in range(side):
        for j in range(side):
            f = jnp.where(c == 0, j, i)
            s = jnp.where(c == 0, i, j)
            d = i * side + j
            for a in range(3):
                kp[f, s, a * share : (a + 1) * share, :] = kin[a * every + d * share : a * every + (d + 1) * share, :]
    copies = []
    for k in range(1, side):
        f, to = on_first(k)
        copy = remote(kp.at[f], kr.at[k], ksend.at[1, k], krecv.at[1, k], dp=to)
        copy.start()
        copies.append(copy)
    for copy in copies:
        copy.wait()
    total = kp[first]
    for k in range(1, side):
        total += kr[k]
    ksum[...] = total
    copies = []
    for k in range(1, side):
        s, to = on_second(k)
        copy = remote(ksum.at[s], kr2.at[k], ksend.at[2, k], krecv.at[2, k], dp=to)
        copy.start()
        copies.append(copy)
    for copy in copies:
        copy.wait()
    total = ksum[second]
    for k in range(1, side):
        total += kr2[k]
    kt[...] = total
    copy = remote(kt, kq, ksend.at[3, 0], krecv.at[3, 0], row=1 - row)
    copy.start()
    copy.wait()
    kt[...] += kq[...]
    store = pltpu.make_async_copy(kt, kg_out, local.at[3])
    store.start()

    for copy in sent:
        copy.wait_send()

    @pl.when(place < 3)
    def _():
        down_copy().wait_send()

    @pl.when(place > 0)
    def _():
        up_copy().wait_send()

    @pl.loop(0, chunks)
    def _(k):
        keep, give = act_copies(k)
        keep.wait()
        give.wait()
        keep, give, low, high = grad_copies(k)
        keep.wait()
        give.wait()
        low.wait_send()
        high.wait_send()
        for of in range(2):
            ref = in_other.at[pl.ds(rows * of + k * ROWS, ROWS)]
            remote(ref, ref, csend.at[of, k], crecv.at[of, k], chan=other + of).wait_recv()

    store.wait()


def shards(images, kernel, cotangent):
    _, height, own, width = images.shape
    share = kernel.shape[1]
    side = math.isqrt(lax.axis_size("dp"))
    rows = height // 2
    chunks = rows // ROWS
    chip, every = 2 * own, 4 * own
    pad_share = round_up(3 * share, 16)
    pad_own = round_up(own, 128)
    lanes = round_up(3 * own, 128)
    dma = pltpu.SemaphoreType.DMA
    scratch = [
        pltpu.VMEM((rows + 2, every, width), BF16),
        pltpu.VMEM((rows, chip, width), BF16),
        pltpu.VMEM((rows + 2, chip, width), BF16),
        pltpu.VMEM((2 * lanes, ROWS * width), BF16),
        pltpu.VMEM((2, 3 * every, lanes), F32),
        pltpu.VMEM(kernel.shape, BF16),
        pltpu.VMEM((3, pad_share, pad_own), F32),
        pltpu.VMEM((2, side, side, 3, pad_share, pad_own), BF16),
        pltpu.VMEM((3 * every, side * side * pad_share), BF16),
        pltpu.VMEM((3 * chip, 3 * every), BF16),
        pltpu.VMEM((3 * every, 3 * chip), BF16),
        pltpu.VMEM((2, rows, own, width), BF16),
        pltpu.VMEM((2, rows, own, width), F32),
        pltpu.VMEM((2, rows, own, width), BF16),
        pltpu.VMEM((3 * every, lanes), F32),
        pltpu.VMEM((side, side, pad_share, lanes), F32),
        pltpu.VMEM((side, side, pad_share, lanes), F32),
        pltpu.VMEM((side, pad_share, lanes), F32),
        pltpu.VMEM((side, pad_share, lanes), F32),
        pltpu.VMEM((pad_share, lanes), F32),
        pltpu.VMEM((pad_share, lanes), F32),
        dma((4,)),
        dma((2, side)), dma((2, side)),
        dma((2, chunks + 1)), dma((2, chunks + 1)),
        dma((2,)), dma((4,)),
        dma((3,)), dma((3,)),
        dma((2,)), dma((2,)),
        dma((chunks,)), dma((chunks,)), dma((chunks,)),
        dma((chunks,)), dma((chunks,)), dma((chunks,)),
        dma((2, chunks)), dma((2, chunks)),
        dma((4, side)), dma((4, side)),
    ]
    hbm = pl.BlockSpec(memory_space=pl.ANY)
    activated, in_own, in_other, terms = pl.pallas_call(
        functools.partial(body, side, own, share, height, width),
        out_shape=(
            jax.ShapeDtypeStruct((height, own, width), BF16),
            jax.ShapeDtypeStruct((height, own, width), F32),
            jax.ShapeDtypeStruct((height, own, width), BF16),
            jax.ShapeDtypeStruct((pad_share, lanes), F32),
        ),
        in_specs=[hbm] * 3,
        out_specs=(hbm,) * 4,
        scratch_shapes=scratch,
        compiler_params=pltpu.CompilerParams(
            collective_id=0, has_side_effects=True, vmem_limit_bytes=56 * 2**20
        ),
        name="conv_block",
    )(images[0], kernel, cotangent[0])
    input_grad = in_own + in_other.astype(F32)
    terms = terms[: 3 * share, : 3 * own].reshape(3, share, 3, own)
    kernel_grad = jnp.transpose(terms, (0, 2, 1, 3)).reshape(9, share, own)
    return activated[None], input_grad[None], kernel_grad


def solution(mesh):
    placed = (P("dp", "row", "chan", None), P(None, "dp", "chan"), P("dp", "row", "chan", None))
    return jax.shard_map(
        shards,
        mesh=mesh,
        in_specs=placed,
        out_specs=(
            P("dp", "row", "chan", None),
            P("dp", "row", "chan", None),
            P(None, "dp", "chan"),
        ),
        check_vma=False,
    )
```

profile of v0, /device:TPU:1, one launch (start us, length us, event | category | flops | bytes accessed | tf_op | source)
XLA Modules:
  0.0 75.2 jit_solution(10601312372900906360)
XLA Ops:
  0.6 68.7 %conv_block.1 = (bf16[64,80,128]{2,1,0:T(8,128)(2,1)}, f32[64,80,128]{2,1,0:T(8,128)}, bf16[64,80,128]{2,1,0:T(8,128)(2,1)}, f32[64,256]{1,0:T(8,128)}) custom-call(bf16[64,80,128]{2,1,0:T(8,128)(2,1)} %bitcast.8, bf16[9,20,80]{2,1,0:T(8,128)(2,1)} %ker.1, bf16[64,80,128]{2,1,0:T(8,128)(2,1)} %bitcast.9), custom_call_target="tpu_custom_call" | custom-call | tf_op jit(solution)/shard_map/conv_block/pallas_call | solution.py:473
  69.4 0.0 copy-start.1
  69.4 0.0 copy-start
  69.4 3.9 %add_bitcast_fusion = f32[1,64,80,128]{3,2,1,0:T(8,128)} fusion(f32[64,80,128]{2,1,0:T(8,128)} %get-tuple-element.8, bf16[64,80,128]{2,1,0:T(8,128)(2,1)} %get-tuple-element.9), kind=kLoop, calls=%fused_computation | loop fusion | flops 1310720 | bytes 6553600 | tf_op jit(solution)/shard_map/broadcast_in_dim | solution.py:492
  73.3 0.0 copy-done.1
  73.3 0.1 reshape.12
  73.4 0.7 copy.7
  74.1 0.0 copy-done
  74.1 1.1 %copy.9 = bf16[1,64,80,128]{3,2,1,0:T(8,128)(2,1)} copy(bf16[1,64,80,128]{3,2,1,0:T(8,128)(2,1)S(1)} %bitcast.10) | data formatting | bytes 2621440
Async XLA Ops:
  69.4 4.0 %copy-start.1 = (f32[64,256]{1,0:T(8,128)S(1)}, f32[64,256]{1,0:T(8,128)}, u32[]{:S(2)}) copy-start(f32[64,256]{1,0:T(8,128)} %get-tuple-element.10) | copy-start | bytes 196612
  69.4 4.7 %copy-start = (bf16[64,80,128]{2,1,0:T(8,128)(2,1)S(1)}, bf16[64,80,128]{2,1,0:T(8,128)(2,1)}, u32[]{:S(2)}) copy-start(bf16[64,80,128]{2,1,0:T(8,128)(2,1)} %get-tuple-element.7) | copy-start | bytes 3932164
where the time goes:
time: 76.2 us; the launch traced here: 75.2 us
  Pallas kernels  68.7 us (90%)
  other arithmetic  3.94 us (5%)
  local copies, waits for them, and re-layouts  1.83 us (2%)
    pallas_call x1, Pallas kernels, shards(): pl.pallas_call(functools.partial(body, side, own, share, height, width),...  68.7 us
    broadcast_in_dim x1, other arithmetic, shards(): return (activated[None], input_grad[None], kernel_grad)  3.94 us

commit v1 on v0

--- a/solution.py
+++ b/solution.py
@@ -12,6 +12,8 @@
 BF16 = jnp.bfloat16
 F32 = jnp.float32
 ROWS = 4
+PARTS = 8
+HELD = 2
 
 
 def round_up(x, m):
@@ -97,6 +99,43 @@
     load_g = pltpu.make_async_copy(cot.at[pl.ds(rows * c, rows)], mine(gs, 0, rows, c), local.at[2])
     load_g.start()
 
+    pl.semaphore_wait(barrier, count)
+
+    pieces = [(rows - ROWS, ROWS + 1), (1, ROWS + 1)]
+    pieces += [(ROWS * k + 2, ROWS) for k in range(1, chunks - 2)]
+    pieces += [(ROWS * (chunks - 2) + 2, ROWS - 2)]
+    sent = []
+
+    def send(*args, **where):
+        copy = remote(*args, **where)
+        copy.start()
+        sent.append(copy)
+
+    def send_piece(to, s):
+        start, n = pieces[s]
+        send(
+            img.at[pl.ds(rows * to + start - 1, n)], mine(xs, start, n, chan),
+            isend.at[to, s], irecv.at[c, s], chan=other + to,
+        )
+
+    send_piece(0, 0)
+    send_piece(1, 1)
+    for to in range(2):
+        send(
+            img.at[pl.ds((height - 1) * (1 - row), 1)], mine(xs, (rows + 1) * row, 1, chan),
+            hsend.at[to], hrecv.at[chan], row=1 - row, chan=2 * to + row,
+        )
+    send(
+        img.at[pl.ds((rows - 1) * (1 - c), rows + 1)], mine(xs, c, rows + 1, chan),
+        bsend.at[0], brecv.at[0], chan=sib,
+    )
+    send(cot.at[pl.ds(rows * (1 - c), rows)], mine(gs, 0, rows, c), bsend.at[1], brecv.at[1], chan=sib)
+    send_piece(0, 1)
+    send_piece(1, 0)
+    for s in range(2, chunks):
+        for to in range(2):
+            send_piece(to, s)
+
     wpk[...] = jnp.zeros_like(wpk)
     for core in range(2):
         s3[core * lanes + 3 * own : (core + 1) * lanes, :] = jnp.zeros((lanes - 3 * own, s3.shape[1]), BF16)
@@ -118,52 +157,12 @@
             wpk[b, a * share : (a + 1) * share, 0:own] = wk[3 * a + b].astype(F32)
     wraw[c, second, first] = wpk[...].astype(BF16)
 
-    pl.semaphore_wait(barrier, count)
-
     gather = []
     for k in range(1, side):
         spot = wraw.at[c, second, first]
         copy = remote(spot, spot, wsend.at[0, k], wrecv.at[0, k], dp=on_first(k)[1])
         copy.start()
         gather.append(copy)
-
-    pieces = [(rows - ROWS, ROWS + 1), (1, ROWS + 1)]
-    pieces += [(ROWS * k + 2, ROWS) for k in range(1, chunks - 2)]
-    pieces += [(ROWS * (chunks - 2) + 2, ROWS - 2)]
-    sent = []
-    for to in range(2):
-        copy = remote(
-            img.at[pl.ds(rows - to, 1)], mine(xs, (rows + 1) * (1 - to), 1, chan),
-            isend.at[to, chunks], irecv.at[c, chunks], chan=other + to,
-        )
-        copy.start()
-        sent.append(copy)
-        copy = remote(
-            img.at[pl.ds((height - 1) * (1 - row), 1)], mine(xs, (rows + 1) * row, 1, chan),
-            hsend.at[to], hrecv.at[chan], row=1 - row, chan=2 * to + row,
-        )
-        copy.start()
-        sent.append(copy)
-    copy = remote(
-        img.at[pl.ds((rows - 1) * (1 - c), rows + 1)], mine(xs, c, rows + 1, chan),
-        bsend.at[0], brecv.at[0], chan=sib,
-    )
-    copy.start()
-    sent.append(copy)
-    for s, (start, n) in enumerate(pieces):
-        for to in range(2):
-            copy = remote(
-                img.at[pl.ds(rows * to + start - 1, n)], mine(xs, start, n, chan),
-                isend.at[to, s], irecv.at[c, s], chan=other + to,
-            )
-            copy.start()
-            sent.append(copy)
-        if s == 0:
-            copy = remote(
-                cot.at[pl.ds(rows * (1 - c), rows)], mine(gs, 0, rows, c), bsend.at[1], brecv.at[1], chan=sib
-            )
-            copy.start()
-            sent.append(copy)
 
     spot = lax.broadcasted_iota(jnp.int32, (1, em.shape[1]), 1)
     owner = jnp.zeros_like(spot)
@@ -184,9 +183,7 @@
         gather.append(copy)
     for k in range(1, side):
         gather[side - 2 + k].wait()
-    copy = remote(wraw.at[c], wraw.at[c], bsend.at[2], brecv.at[2], chan=sib)
-    copy.start()
-    sent.append(copy)
+    send(wraw.at[c], wraw.at[c], bsend.at[2], brecv.at[2], chan=sib)
     remote(wraw.at[c], wraw.at[1 - c], bsend.at[2], brecv.at[2], chan=sib).wait_recv()
 
     wide = 2 * wraw.shape[-1]
@@ -221,15 +218,12 @@
     load_g.wait()
     for which, ref in ((0, mine(xs, 1 - c, rows + 1, sib)), (1, mine(gs, 0, rows, 1 - c))):
         remote(ref, ref, bsend.at[which], brecv.at[which], chan=sib).wait_recv()
-    for of in range(2):
-        ref = mine(xs, (rows + 1) * (1 - c), 1, other + of)
-        remote(ref, ref, isend.at[of, chunks], irecv.at[of, chunks], chan=other + of).wait_recv()
-
-    @pl.when(c != row)
-    def _():
-        for g in range(4):
-            ref = mine(xs, (rows + 1) * c, 1, g)
-            remote(ref, ref, hsend.at[0], hrecv.at[g], row=1 - row, chan=g).wait_recv()
+    def border():
+        at = pl.ds(pl.multiple_of(own * other, 16), chip)
+        return remote(
+            xs.at[jnp.where(c == 0, rows, 1), at], xs.at[jnp.where(c == 0, 0, rows + 1), at],
+            bsend.at[3], brecv.at[3], chan=sib,
+        )
 
     def await_rows(s, start, n):
         for of in range(2):
@@ -243,6 +237,16 @@
 
     def up_copy():
         return remote(ss.at[1], ss.at[rows + 1], ssend.at[1], srecv.at[1], row=row - (1 - c), chan=sib)
+
+    def trade():
+        return remote(acc.at[1 - c], kin, ksend.at[0, 0], krecv.at[0, 0], chan=sib)
+
+    def plane_copies():
+        made = []
+        for k in range(1, side):
+            f, to = on_first(k)
+            made.append(remote(kp.at[f], kr.at[k], ksend.at[1, k], krecv.at[1, k], dp=to))
+        return made
 
     def act_copies(k):
         at = pl.ds(k * ROWS, ROWS)
@@ -252,12 +256,18 @@
             remote(ab.at[1 - c, at], act_out.at[to], asend.at[k], arecv.at[k], chan=sib),
         )
 
-    def grad_copies(k):
+    def near_copies(k):
         at = pl.ds(k * ROWS, ROWS)
         to = pl.ds(rows * c + k * ROWS, ROWS)
         return (
             pltpu.make_async_copy(pf.at[c, at], in_own.at[to], plocal.at[k]),
             remote(pf.at[1 - c, at], in_own.at[to], psend.at[k], precv.at[k], chan=sib),
+        )
+
+    def far_copies(k):
+        at = pl.ds(k * ROWS, ROWS)
+        to = pl.ds(rows * c + k * ROWS, ROWS)
+        return (
             remote(pb.at[0, at], in_other.at[to], csend.at[0, k], crecv.at[c, k], chan=other),
             remote(pb.at[1, at], in_other.at[to], csend.at[1, k], crecv.at[c, k], chan=other + 1),
         )
@@ -312,11 +322,25 @@
 
     @pl.loop(0, chunks + 3)
     def _(s):
-        for fixed in (0, 1, chunks - 1):
-
-            @pl.when(s == fixed)
-            def _():
-                await_rows(fixed, *pieces[fixed])
+        @pl.when(s < 2)
+        def _():
+            piece = jnp.where(s == 0, c, 1 - c)
+            await_rows(piece, jnp.where(piece == 0, rows - ROWS, 1), ROWS + 1)
+
+        @pl.when(s == 0)
+        def _():
+            border().start()
+            border().wait_recv()
+
+        @pl.when(jnp.logical_and(s == 1, c != row))
+        def _():
+            for g in range(4):
+                ref = mine(xs, (rows + 1) * c, 1, g)
+                remote(ref, ref, hsend.at[0], hrecv.at[g], row=1 - row, chan=g).wait_recv()
+
+        @pl.when(s == chunks - 1)
+        def _():
+            await_rows(chunks - 1, *pieces[chunks - 1])
 
         @pl.when(jnp.logical_and(s > 1, s < chunks - 1))
         def _():
@@ -324,18 +348,22 @@
 
         @pl.when(s < chunks)
         def _():
-            k = lax.rem(s + chunks - 1, chunks)
+            k = jnp.where(s < 2, jnp.where(s == c, chunks - 1, 0), s - 1)
             forward(k)
             for copy in act_copies(k):
                 copy.start()
 
-        @pl.when(jnp.logical_and(s == 0, place < 3))
+        @pl.when(jnp.logical_and(s == c, place < 3))
         def _():
             down_copy().start()
 
-        @pl.when(jnp.logical_and(s == 1, place > 0))
+        @pl.when(jnp.logical_and(s == 1 - c, place > 0))
         def _():
             up_copy().start()
+
+        @pl.when(s == chunks - 1)
+        def _():
+            trade().start()
 
         @pl.when(jnp.logical_and(s == chunks + 1, place < 3))
         def _():
@@ -349,30 +377,31 @@
         def _():
             k = lax.rem(s - 2, chunks)
             backward(k)
-            for copy in grad_copies(k):
+            for copy in near_copies(k):
                 copy.start()
 
-        @pl.when(s == chunks - 1)
-        def _():
-            remote(acc.at[1 - c], kin, ksend.at[0, 0], krecv.at[0, 0], chan=sib).start()
-
-    trade = remote(acc.at[1 - c], kin, ksend.at[0, 0], krecv.at[0, 0], chan=sib)
-    trade.wait()
-    kin[...] += acc[c]
-    for i in range(side):
-        for j in range(side):
-            f = jnp.where(c == 0, j, i)
-            s = jnp.where(c == 0, i, j)
-            d = i * side + j
-            for a in range(3):
-                kp[f, s, a * share : (a + 1) * share, :] = kin[a * every + d * share : a * every + (d + 1) * share, :]
-    copies = []
-    for k in range(1, side):
-        f, to = on_first(k)
-        copy = remote(kp.at[f], kr.at[k], ksend.at[1, k], krecv.at[1, k], dp=to)
-        copy.start()
-        copies.append(copy)
-    for copy in copies:
+            @pl.when(s < chunks + 3 - HELD)
+            def _():
+                for copy in far_copies(k):
+                    copy.start()
+
+        @pl.when(s == chunks)
+        def _():
+            trade().wait()
+            kin[...] += acc[c]
+            for i in range(side):
+                for j in range(side):
+                    f = jnp.where(c == 0, j, i)
+                    to = jnp.where(c == 0, i, j)
+                    d = i * side + j
+                    for a in range(3):
+                        kp[f, to, a * share : (a + 1) * share, :] = kin[
+                            a * every + d * share : a * every + (d + 1) * share, :
+                        ]
+            for copy in plane_copies():
+                copy.start()
+
+    for copy in plane_copies():
         copy.wait()
     total = kp[first]
     for k in range(1, side):
@@ -392,13 +421,16 @@
     kt[...] = total
     copy = remote(kt, kq, ksend.at[3, 0], krecv.at[3, 0], row=1 - row)
     copy.start()
+    for s in range(chunks + 3 - HELD, chunks + 3):
+        for far in far_copies((s - 2) % chunks):
+            far.start()
     copy.wait()
-    kt[...] += kq[...]
-    store = pltpu.make_async_copy(kt, kg_out, local.at[3])
-    store.start()
+    kg_out[...] = kt[...] + kq[...]
 
     for copy in sent:
         copy.wait_send()
+
+    border().wait_send()
 
     @pl.when(place < 3)
     def _():
@@ -413,16 +445,36 @@
         keep, give = act_copies(k)
         keep.wait()
         give.wait()
-        keep, give, low, high = grad_copies(k)
+        keep, give = near_copies(k)
         keep.wait()
         give.wait()
-        low.wait_send()
-        high.wait_send()
+        for copy in far_copies(k):
+            copy.wait_send()
         for of in range(2):
             ref = in_other.at[pl.ds(rows * of + k * ROWS, ROWS)]
             remote(ref, ref, csend.at[of, k], crecv.at[of, k], chan=other + of).wait_recv()
 
-    store.wait()
+
+def finish(own, share, act, in_own, in_other, terms, act_out, grad_out, kg_out, grad, kg, sems):
+    keep = pltpu.make_async_copy(act, act_out, sems.at[0])
+    keep.start()
+    step = in_own.shape[0] // PARTS
+    copies = []
+    for p in range(PARTS):
+        at = pl.ds(p * step, step)
+        grad[at] = in_own[at] + in_other[at].astype(F32)
+        copy = pltpu.make_async_copy(grad.at[at], grad_out.at[at], sems.at[2 + p])
+        copy.start()
+        copies.append(copy)
+    for a in range(3):
+        for b in range(3):
+            kg[3 * a + b] = terms[a * share : (a + 1) * share, b * own : (b + 1) * own]
+    last = pltpu.make_async_copy(kg, kg_out, sems.at[1])
+    last.start()
+    keep.wait()
+    for copy in copies:
+        copy.wait()
+    last.wait()
 
 
 def shards(images, kernel, cotangent):
@@ -458,11 +510,11 @@
         pltpu.VMEM((side, pad_share, lanes), F32),
         pltpu.VMEM((pad_share, lanes), F32),
         pltpu.VMEM((pad_share, lanes), F32),
-        dma((4,)),
+        dma((3,)),
         dma((2, side)), dma((2, side)),
-        dma((2, chunks + 1)), dma((2, chunks + 1)),
+        dma((2, chunks)), dma((2, chunks)),
         dma((2,)), dma((4,)),
-        dma((3,)), dma((3,)),
+        dma((4,)), dma((4,)),
         dma((2,)), dma((2,)),
         dma((chunks,)), dma((chunks,)), dma((chunks,)),
         dma((chunks,)), dma((chunks,)), dma((chunks,)),
@@ -470,25 +522,40 @@
         dma((4, side)), dma((4, side)),
     ]
     hbm = pl.BlockSpec(memory_space=pl.ANY)
+    vmem = pl.BlockSpec(memory_space=pltpu.VMEM)
     activated, in_own, in_other, terms = pl.pallas_call(
         functools.partial(body, side, own, share, height, width),
         out_shape=(
-            jax.ShapeDtypeStruct((height, own, width), BF16),
-            jax.ShapeDtypeStruct((height, own, width), F32),
-            jax.ShapeDtypeStruct((height, own, width), BF16),
-            jax.ShapeDtypeStruct((pad_share, lanes), F32),
+            pltpu.VMEM((height, own, width), BF16),
+            pltpu.VMEM((height, own, width), F32),
+            pltpu.VMEM((height, own, width), BF16),
+            pltpu.VMEM((pad_share, lanes), F32),
         ),
         in_specs=[hbm] * 3,
-        out_specs=(hbm,) * 4,
+        out_specs=(vmem,) * 4,
         scratch_shapes=scratch,
         compiler_params=pltpu.CompilerParams(
-            collective_id=0, has_side_effects=True, vmem_limit_bytes=56 * 2**20
+            collective_id=0, has_side_effects=True, vmem_limit_bytes=44 * 2**20
         ),
         name="conv_block",
     )(images[0], kernel, cotangent[0])
-    input_grad = in_own + in_other.astype(F32)
-    terms = terms[: 3 * share, : 3 * own].reshape(3, share, 3, own)
-    kernel_grad = jnp.transpose(terms, (0, 2, 1, 3)).reshape(9, share, own)
+    activated, input_grad, kernel_grad = pl.pallas_call(
+        functools.partial(finish, own, share),
+        out_shape=(
+            jax.ShapeDtypeStruct((height, own, width), BF16),
+            jax.ShapeDtypeStruct((height, own, width), F32),
+            jax.ShapeDtypeStruct((9, share, own), F32),
+        ),
+        in_specs=[vmem] * 4,
+        out_specs=(hbm, hbm, hbm),
+        scratch_shapes=[
+            pltpu.VMEM((height, own, width), F32),
+            pltpu.VMEM((9, share, own), F32),
+            dma((2 + PARTS,)),
+        ],
+        compiler_params=pltpu.CompilerParams(vmem_limit_bytes=16 * 2**20),
+        name="results",
+    )(activated, in_own, in_other, terms)
     return activated[None], input_grad[None], kernel_grad
 
 

time: 76.2 us -> 76.9 us (level); the launches traced: 75.2 us -> 76.7 us
  other arithmetic: 3.94 us -> 0 us
  Pallas kernels: 68.7 us -> 72.6 us
  local copies, waits for them, and re-layouts: 1.83 us -> 3.44 us
    broadcast_in_dim x1 -> x0, other arithmetic: 3.94 us -> none  [shards(): return (activated[None], input_grad[None], kernel_grad)]
    unnamed x5 -> x6, local copies, waits for them, and re-layouts: 1.06 us -> 3.44 us
    pallas_call x0 -> x1, Pallas kernels: none -> 2.02 us  [shards(): pl.pallas_call(functools.partial(finish, own, share), out_shape=(jax.Shap...]
    pallas_call x1, Pallas kernels: 68.7 us -> 70.6 us  [shards(): pl.pallas_call(functools.partial(body, side, own, share, height, width),...]
where the time goes in v1:
time: 76.9 us; the launch traced here: 76.7 us
  Pallas kernels  72.6 us (94%)
  local copies, waits for them, and re-layouts  3.44 us (4%)
    pallas_call x1, Pallas kernels, shards(): pl.pallas_call(functools.partial(body, side, own, share, height, width),...  70.6 us
    unnamed x6, local copies, waits for them, and re-layouts  3.44 us
    pallas_call x1, Pallas kernels, shards(): pl.pallas_call(functools.partial(finish, own, share), out_shape=(jax.Shap...  2.02 us

profile of v1, /device:TPU:1, one launch (start us, length us, event | category | flops | bytes accessed | tf_op | source)
XLA Modules:
  0.0 76.7 jit_solution(8571983286136570356)
XLA Ops:
  0.6 0.0 copy-start
  0.6 1.3 %copy-done = bf16[1,64,80,128]{3,2,1,0:T(8,128)(2,1)S(1)} copy-done((bf16[1,64,80,128]{3,2,1,0:T(8,128)(2,1)S(1)}, bf16[1,64,80,128]{3,2,1,0:T(8,128)(2,1)}, u32[]{:S(2)}) %copy-start) | copy-done | bytes 1310744
  1.9 0.0 copy-start.1
  1.9 1.3 %copy-done.1 = bf16[1,64,80,128]{3,2,1,0:T(8,128)(2,1)S(1)} copy-done((bf16[1,64,80,128]{3,2,1,0:T(8,128)(2,1)S(1)}, bf16[1,64,80,128]{3,2,1,0:T(8,128)(2,1)}, u32[]{:S(2)}) %copy-start.1) | copy-done | bytes 1310744
  3.3 0.0 copy-start.2
  3.3 0.8 %copy-done.2 = bf16[9,20,80]{2,1,0:T(8,128)(2,1)S(1)} copy-done((bf16[9,20,80]{2,1,0:T(8,128)(2,1)S(1)}, bf16[9,20,80]{2,1,0:T(8,128)(2,1)}, u32[]{:S(2)}) %copy-start.2) | copy-done | bytes 28824
  4.1 70.6 %conv_block.1 = (bf16[64,80,128]{2,1,0:T(8,128)(2,1)S(1)}, f32[64,80,128]{2,1,0:T(8,128)S(1)}, bf16[64,80,128]{2,1,0:T(8,128)(2,1)S(1)}, f32[64,256]{1,0:T(8,128)S(1)}) custom-call(bf16[64,80,128]{2,1,0:T(8,128)(2,1)S(1)} %bitcast.4, bf16[9,20,80]{2,1,0:T(8,128)(2,1)S(1)} %copy-done.2, bf16[64,80,128]{2,1,0:T(8,128)(2,1)S(1)} %bitcast.5), custom_call_target="tpu_custom_call" | custom-call | tf_op jit(solution)/shard_map/conv_block/pallas_call | solution.py:526
  74.7 2.0 %results.1 = (bf16[64,80,128]{2,1,0:T(8,128)(2,1)}, f32[64,80,128]{2,1,0:T(8,128)}, f32[9,20,80]{2,1,0:T(8,128)}) custom-call(bf16[64,80,128]{2,1,0:T(8,128)(2,1)S(1)} %get-tuple-element.10.act, f32[64,80,128]{2,1,0:T(8,128)S(1)} %get-tuple-element.11.in_own, bf16[64,80,128]{2,1,0:T(8,128)(2,1)S(1)} %get-tuple-element.12.in_other, ...), custom_call_target="tpu_custom_call" | custom-call | tf_op jit(solution)/shard_map/results/pallas_call | solution.py:542
Async XLA Ops:
  0.6 1.3 %copy-start = (bf16[1,64,80,128]{3,2,1,0:T(8,128)(2,1)S(1)}, bf16[1,64,80,128]{3,2,1,0:T(8,128)(2,1)}, u32[]{:S(2)}) copy-start(bf16[1,64,80,128]{3,2,1,0:T(8,128)(2,1)} %param.3) | copy-start | bytes 3932164
  1.9 1.3 %copy-start.1 = (bf16[1,64,80,128]{3,2,1,0:T(8,128)(2,1)S(1)}, bf16[1,64,80,128]{3,2,1,0:T(8,128)(2,1)}, u32[]{:S(2)}) copy-start(bf16[1,64,80,128]{3,2,1,0:T(8,128)(2,1)} %param.5) | copy-start | bytes 3932164
  3.3 0.8 %copy-start.2 = (bf16[9,20,80]{2,1,0:T(8,128)(2,1)S(1)}, bf16[9,20,80]{2,1,0:T(8,128)(2,1)}, u32[]{:S(2)}) copy-start(bf16[9,20,80]{2,1,0:T(8,128)(2,1)} %ker.1) | copy-start | bytes 86404

commit v2 on v1

--- a/solution.py
+++ b/solution.py
@@ -12,8 +12,8 @@
 BF16 = jnp.bfloat16
 F32 = jnp.float32
 ROWS = 4
-PARTS = 8
-HELD = 2
+PARTS = 4
+HELD = 1
 
 
 def round_up(x, m):
@@ -39,9 +39,9 @@
 def body(
     side, own, share, height, width,
     img, ker, cot,
-    act_out, in_own, in_other, kg_out,
+    act_out, grad_out, kg_out,
     xs, gs, ss, s3, acc, wk, wpk, wraw, em, wf, wb, ab, pf, pb,
-    kin, kp, kr, ksum, kr2, kt, kq,
+    arrived, kin, kp, kr, ksum, kr2, kt, kq,
     local, wsend, wrecv, isend, irecv, hsend, hrecv, bsend, brecv,
     ssend, srecv, asend, arecv, alocal, plocal, psend, precv, csend, crecv, ksend, krecv,
 ):
@@ -260,16 +260,16 @@
         at = pl.ds(k * ROWS, ROWS)
         to = pl.ds(rows * c + k * ROWS, ROWS)
         return (
-            pltpu.make_async_copy(pf.at[c, at], in_own.at[to], plocal.at[k]),
-            remote(pf.at[1 - c, at], in_own.at[to], psend.at[k], precv.at[k], chan=sib),
+            pltpu.make_async_copy(pf.at[c, at], grad_out.at[to], plocal.at[k]),
+            remote(pf.at[1 - c, at], grad_out.at[to], psend.at[k], precv.at[k], chan=sib),
         )
 
     def far_copies(k):
         at = pl.ds(k * ROWS, ROWS)
         to = pl.ds(rows * c + k * ROWS, ROWS)
         return (
-            remote(pb.at[0, at], in_other.at[to], csend.at[0, k], crecv.at[c, k], chan=other),
-            remote(pb.at[1, at], in_other.at[to], csend.at[1, k], crecv.at[c, k], chan=other + 1),
+            remote(pb.at[0, at], arrived.at[to], csend.at[0, k], crecv.at[c, k], chan=other),
+            remote(pb.at[1, at], arrived.at[to], csend.at[1, k], crecv.at[c, k], chan=other + 1),
         )
 
     def three(ref, start):
@@ -385,7 +385,7 @@
                 for copy in far_copies(k):
                     copy.start()
 
-        @pl.when(s == chunks)
+        @pl.when(s == chunks - 1)
         def _():
             trade().wait()
             kin[...] += acc[c]
@@ -427,9 +427,19 @@
     copy.wait()
     kg_out[...] = kt[...] + kq[...]
 
+    @pl.loop(1, chunks + 1)
+    def _(k):
+        k = lax.rem(k, chunks)
+        for copy in near_copies(k):
+            copy.wait()
+        for of in range(2):
+            at = pl.ds(rows * of + k * ROWS, ROWS)
+            ref = arrived.at[at]
+            remote(ref, ref, csend.at[of, k], crecv.at[of, k], chan=other + of).wait_recv()
+            grad_out[at] += arrived[at].astype(F32)
+
     for copy in sent:
         copy.wait_send()
-
     border().wait_send()
 
     @pl.when(place < 3)
@@ -442,36 +452,26 @@
 
     @pl.loop(0, chunks)
     def _(k):
-        keep, give = act_copies(k)
-        keep.wait()
-        give.wait()
-        keep, give = near_copies(k)
-        keep.wait()
-        give.wait()
+        for copy in act_copies(k):
+            copy.wait()
         for copy in far_copies(k):
             copy.wait_send()
-        for of in range(2):
-            ref = in_other.at[pl.ds(rows * of + k * ROWS, ROWS)]
-            remote(ref, ref, csend.at[of, k], crecv.at[of, k], chan=other + of).wait_recv()
-
-
-def finish(own, share, act, in_own, in_other, terms, act_out, grad_out, kg_out, grad, kg, sems):
-    keep = pltpu.make_async_copy(act, act_out, sems.at[0])
-    keep.start()
-    step = in_own.shape[0] // PARTS
+
+
+def finish(own, share, act, grad, terms, act_out, grad_out, kg_out, kg, sems):
+    step = grad.shape[0] // PARTS
     copies = []
     for p in range(PARTS):
         at = pl.ds(p * step, step)
-        grad[at] = in_own[at] + in_other[at].astype(F32)
-        copy = pltpu.make_async_copy(grad.at[at], grad_out.at[at], sems.at[2 + p])
+        copies.append(pltpu.make_async_copy(grad.at[at], grad_out.at[at], sems.at[p, 0]))
+        copies.append(pltpu.make_async_copy(act.at[at], act_out.at[at], sems.at[p, 1]))
+    for copy in copies:
         copy.start()
-        copies.append(copy)
     for a in range(3):
         for b in range(3):
             kg[3 * a + b] = terms[a * share : (a + 1) * share, b * own : (b + 1) * own]
-    last = pltpu.make_async_copy(kg, kg_out, sems.at[1])
+    last = pltpu.make_async_copy(kg, kg_out, sems.at[PARTS, 0])
     last.start()
-    keep.wait()
     for copy in copies:
         copy.wait()
     last.wait()
@@ -503,6 +503,7 @@
         pltpu.VMEM((2, rows, own, width), BF16),
         pltpu.VMEM((2, rows, own, width), F32),
         pltpu.VMEM((2, rows, own, width), BF16),
+        pltpu.VMEM((height, own, width), BF16),
         pltpu.VMEM((3 * every, lanes), F32),
         pltpu.VMEM((side, side, pad_share, lanes), F32),
         pltpu.VMEM((side, side, pad_share, lanes), F32),
@@ -523,19 +524,18 @@
     ]
     hbm = pl.BlockSpec(memory_space=pl.ANY)
     vmem = pl.BlockSpec(memory_space=pltpu.VMEM)
-    activated, in_own, in_other, terms = pl.pallas_call(
+    activated, input_grad, terms = pl.pallas_call(
         functools.partial(body, side, own, share, height, width),
         out_shape=(
             pltpu.VMEM((height, own, width), BF16),
             pltpu.VMEM((height, own, width), F32),
-            pltpu.VMEM((height, own, width), BF16),
             pltpu.VMEM((pad_share, lanes), F32),
         ),
         in_specs=[hbm] * 3,
-        out_specs=(vmem,) * 4,
+        out_specs=(vmem,) * 3,
         scratch_shapes=scratch,
         compiler_params=pltpu.CompilerParams(
-            collective_id=0, has_side_effects=True, vmem_limit_bytes=44 * 2**20
+            collective_id=0, has_side_effects=True, vmem_limit_bytes=56 * 2**20
         ),
         name="conv_block",
     )(images[0], kernel, cotangent[0])
@@ -546,16 +546,12 @@
             jax.ShapeDtypeStruct((height, own, width), F32),
             jax.ShapeDtypeStruct((9, share, own), F32),
         ),
-        in_specs=[vmem] * 4,
+        in_specs=[vmem] * 3,
         out_specs=(hbm, hbm, hbm),
-        scratch_shapes=[
-            pltpu.VMEM((height, own, width), F32),
-            pltpu.VMEM((9, share, own), F32),
-            dma((2 + PARTS,)),
-        ],
+        scratch_shapes=[pltpu.VMEM((9, share, own), F32), dma((PARTS + 1, 2))],
         compiler_params=pltpu.CompilerParams(vmem_limit_bytes=16 * 2**20),
         name="results",
-    )(activated, in_own, in_other, terms)
+    )(activated, input_grad, terms)
     return activated[None], input_grad[None], kernel_grad
 
 

time: 76.9 us -> 70.2 us (0.913)
  local copies, waits for them, and re-layouts: 3.44 us -> 0 us
  Pallas kernels: 72.6 us -> 69.5 us
    unnamed x6 -> x0, local copies, waits for them, and re-layouts: 3.44 us -> none
    pallas_call x1, Pallas kernels: 70.6 us -> 67.5 us  [shards(): pl.pallas_call(functools.partial(body, side, own, share, height, width),...]
where the time goes in v2:
time: 70.2 us; the launch traced here: 70.1 us
  Pallas kernels  69.5 us (99%)
    pallas_call x1, Pallas kernels, shards(): pl.pallas_call(functools.partial(body, side, own, share, height, width),...  67.5 us
    pallas_call x1, Pallas kernels, shards(): pl.pallas_call(functools.partial(finish, own, share), out_shape=(jax.Shap...  2.02 us

profile of v2, /device:TPU:1, one launch (start us, length us, event | category | flops | bytes accessed | tf_op | source)
XLA Modules:
  0.0 70.1 jit_solution(8544987729646056574)
XLA Ops:
  0.6 67.5 %conv_block.1 = (bf16[64,80,128]{2,1,0:T(8,128)(2,1)S(1)}, f32[64,80,128]{2,1,0:T(8,128)S(1)}, f32[64,256]{1,0:T(8,128)S(1)}) custom-call(bf16[64,80,128]{2,1,0:T(8,128)(2,1)} %bitcast.4, bf16[9,20,80]{2,1,0:T(8,128)(2,1)} %ker.1, bf16[64,80,128]{2,1,0:T(8,128)(2,1)} %bitcast.5), custom_call_target="tpu_custom_call" | custom-call | tf_op jit(solution)/shard_map/conv_block/pallas_call | solution.py:527
  68.1 2.0 %results.1 = (bf16[64,80,128]{2,1,0:T(8,128)(2,1)}, f32[64,80,128]{2,1,0:T(8,128)}, f32[9,20,80]{2,1,0:T(8,128)}) custom-call(bf16[64,80,128]{2,1,0:T(8,128)(2,1)S(1)} %get-tuple-element.9.act, f32[64,80,128]{2,1,0:T(8,128)S(1)} %get-tuple-element.10.grad, f32[64,256]{1,0:T(8,128)S(1)} %get-tuple-element.11.terms), custom_call_target="tpu_custom_call" | custom-call | tf_op jit(solution)/shard_map/results/pallas_call | solution.py:542

commit v3 on v2

--- a/solution.py
+++ b/solution.py
@@ -44,13 +44,14 @@
     arrived, kin, kp, kr, ksum, kr2, kt, kq,
     local, wsend, wrecv, isend, irecv, hsend, hrecv, bsend, brecv,
     ssend, srecv, asend, arecv, alocal, plocal, psend, precv, csend, crecv, ksend, krecv,
+    fsend, frecv, near_ready, far_ready,
 ):
     rows = height // 2
     chunks = rows // ROWS
     chip = 2 * own
     every = 4 * own
-    pad_share = wpk.shape[1]
-    lanes = s3.shape[0] // 2
+    pad_share = wpk.shape[0]
+    lanes = s3.shape[1] // 2
 
     dp = lax.axis_index("dp")
     chan = lax.axis_index("chan")
@@ -75,17 +76,17 @@
         return s, first * step_first + s * step_second
 
     barrier = pltpu.get_barrier_semaphore()
-    count = 0
-    for k in range(1, 4):
-        pl.semaphore_signal(barrier, inc=1, device_id={"chan": lax.rem(chan + k, 4)}, device_id_type=MESH)
-        count += 1
-    for g in range(4):
-        pl.semaphore_signal(barrier, inc=1, device_id={"row": 1 - row, "chan": g}, device_id_type=MESH)
-        count += 1
+    pl.semaphore_signal(barrier, inc=1, device_id={"chan": other + 1}, device_id_type=MESH)
+
+    @pl.when(c == 0)
+    def _():
+        pl.semaphore_signal(barrier, inc=1, device_id={"chan": sib}, device_id_type=MESH)
+
+    for to in range(2):
+        pl.semaphore_signal(barrier, inc=1, device_id={"row": 1 - row, "chan": 2 * to}, device_id_type=MESH)
     for k in range(1, side):
-        pl.semaphore_signal(barrier, inc=1, device_id={"dp": on_first(k)[1]}, device_id_type=MESH)
-        pl.semaphore_signal(barrier, inc=1, device_id={"dp": on_second(k)[1]}, device_id_type=MESH)
-        count += 2
+        for to in (on_first(k)[1], on_second(k)[1]):
+            pl.semaphore_signal(barrier, inc=1, device_id={"dp": to, "chan": 2 * l}, device_id_type=MESH)
 
     def mine(ref, first_row, n, g):
         return ref.at[pl.ds(first_row, n), pl.ds(pl.multiple_of(own * g, 16), own)]
@@ -99,7 +100,14 @@
     load_g = pltpu.make_async_copy(cot.at[pl.ds(rows * c, rows)], mine(gs, 0, rows, c), local.at[2])
     load_g.start()
 
-    pl.semaphore_wait(barrier, count)
+    @pl.when(c == 1)
+    def _():
+        pl.semaphore_wait(barrier, 3)
+        pl.semaphore_signal(near_ready, inc=1, device_id={"chan": sib}, device_id_type=MESH)
+
+    @pl.when(c == 0)
+    def _():
+        pl.semaphore_wait(near_ready, 1)
 
     pieces = [(rows - ROWS, ROWS + 1), (1, ROWS + 1)]
     pieces += [(ROWS * k + 2, ROWS) for k in range(1, chunks - 2)]
@@ -120,11 +128,6 @@
 
     send_piece(0, 0)
     send_piece(1, 1)
-    for to in range(2):
-        send(
-            img.at[pl.ds((height - 1) * (1 - row), 1)], mine(xs, (rows + 1) * row, 1, chan),
-            hsend.at[to], hrecv.at[chan], row=1 - row, chan=2 * to + row,
-        )
     send(
         img.at[pl.ds((rows - 1) * (1 - c), rows + 1)], mine(xs, c, rows + 1, chan),
         bsend.at[0], brecv.at[0], chan=sib,
@@ -132,30 +135,24 @@
     send(cot.at[pl.ds(rows * (1 - c), rows)], mine(gs, 0, rows, c), bsend.at[1], brecv.at[1], chan=sib)
     send_piece(0, 1)
     send_piece(1, 0)
-    for s in range(2, chunks):
-        for to in range(2):
-            send_piece(to, s)
+    for to in range(2):
+        send_piece(to, 2)
 
     wpk[...] = jnp.zeros_like(wpk)
-    for core in range(2):
-        s3[core * lanes + 3 * own : (core + 1) * lanes, :] = jnp.zeros((lanes - 3 * own, s3.shape[1]), BF16)
-
-    @pl.when(jnp.logical_and(c == 0, row == 0))
-    def _():
-        xs[0] = jnp.zeros(xs.shape[1:], BF16)
-        ss[0] = jnp.zeros(ss.shape[1:], BF16)
-
-    @pl.when(jnp.logical_and(c == 1, row == 1))
-    def _():
-        xs[rows + 1] = jnp.zeros(xs.shape[1:], BF16)
-        ss[rows + 1] = jnp.zeros(ss.shape[1:], BF16)
-
-    acc[...] = jnp.zeros_like(acc)
     load_k.wait()
     for b in range(3):
         for a in range(3):
-            wpk[b, a * share : (a + 1) * share, 0:own] = wk[3 * a + b].astype(F32)
+            wpk[a * share : (a + 1) * share, b * own : (b + 1) * own] = wk[3 * a + b].astype(F32)
     wraw[c, second, first] = wpk[...].astype(BF16)
+
+    @pl.when(c == 0)
+    def _():
+        pl.semaphore_wait(barrier, 4 + 4 * (side - 1))
+        pl.semaphore_signal(far_ready, inc=1, device_id={"chan": sib}, device_id_type=MESH)
+
+    @pl.when(c == 1)
+    def _():
+        pl.semaphore_wait(far_ready, 1)
 
     gather = []
     for k in range(1, side):
@@ -164,6 +161,29 @@
         copy.start()
         gather.append(copy)
 
+    for to in range(2):
+        send(
+            img.at[pl.ds((height - 1) * (1 - row), 1)], mine(xs, (rows + 1) * row, 1, chan),
+            hsend.at[to], hrecv.at[chan], row=1 - row, chan=2 * to + row,
+        )
+    for s in range(3, chunks):
+        for to in range(2):
+            send_piece(to, s)
+
+    for core in range(2):
+        s3[:, core * lanes + 3 * own : (core + 1) * lanes, :] = jnp.zeros((chunks, lanes - 3 * own, s3.shape[2]), BF16)
+
+    @pl.when(jnp.logical_and(c == 0, row == 0))
+    def _():
+        xs[0] = jnp.zeros(xs.shape[1:], BF16)
+        ss[0] = jnp.zeros(ss.shape[1:], BF16)
+
+    @pl.when(jnp.logical_and(c == 1, row == 1))
+    def _():
+        xs[rows + 1] = jnp.zeros(xs.shape[1:], BF16)
+        ss[rows + 1] = jnp.zeros(ss.shape[1:], BF16)
+
+    acc[...] = jnp.zeros_like(acc)
     spot = lax.broadcasted_iota(jnp.int32, (1, em.shape[1]), 1)
     owner = jnp.zeros_like(spot)
     for k in range(1, side * side):
@@ -174,45 +194,38 @@
     target = jnp.where(within < 3 * share, target, -1)
     em[...] = (lax.broadcasted_iota(jnp.int32, em.shape, 0) == target).astype(F32).astype(BF16)
 
+    for copy in gather:
+        copy.wait()
+    spot = wraw.at[c, second]
+    gather = [remote(spot, spot, wsend.at[1, k], wrecv.at[1, k], dp=on_second(k)[1]) for k in range(1, side)]
+    for copy in gather:
+        copy.start()
+    send(spot, spot, fsend.at[0], frecv.at[0], chan=sib)
     for k in range(1, side):
         gather[k - 1].wait()
-    for k in range(1, side):
-        spot = wraw.at[c, second]
-        copy = remote(spot, spot, wsend.at[1, k], wrecv.at[1, k], dp=on_second(k)[1])
-        copy.start()
-        gather.append(copy)
-    for k in range(1, side):
-        gather[side - 2 + k].wait()
-    send(wraw.at[c], wraw.at[c], bsend.at[2], brecv.at[2], chan=sib)
-    remote(wraw.at[c], wraw.at[1 - c], bsend.at[2], brecv.at[2], chan=sib).wait_recv()
-
-    wide = 2 * wraw.shape[-1]
-    fold = (
-        lax.broadcasted_iota(jnp.int32, (wide, 3 * chip), 0),
-        lax.broadcasted_iota(jnp.int32, (wide, 3 * chip), 1),
-    )
-    half = wide // 2
-    core_of = (fold[0] >= half).astype(jnp.int32)
-    inside = fold[0] - core_of * half
-    for b in range(3):
-        blocks = []
-        for core in range(2):
-            order = [(i, j) if core == 0 else (j, i) for i in range(side) for j in range(side)]
-            blocks.append(jnp.concatenate([wraw[core, i, j, b] for i, j in order], axis=0))
-        taps = jnp.dot(em[...], jnp.concatenate(blocks, axis=1), preferred_element_type=F32)
+        spot = wraw.at[c, lax.rem(second + side - k, side)]
+        send(spot, spot, fsend.at[k], frecv.at[k], chan=sib)
+    for k in range(side):
+        spot = wraw.at[1 - c, k]
+        remote(spot, spot, fsend.at[k], frecv.at[k], chan=sib).wait_recv()
+
+    for core in range(2):
+        order = [(i, j) if core == 0 else (j, i) for i in range(side) for j in range(side)]
+        blocks = jnp.concatenate([wraw[core, i, j] for i, j in order], axis=0)
+        taps = jnp.dot(em[...], blocks, preferred_element_type=F32)
         turned = jnp.transpose(taps).astype(BF16)
-        for core in range(2):
-            wf[b * chip + core * own : b * chip + (core + 1) * own, :] = turned[core * half : core * half + own]
+        for b in range(3):
+            wf[b * chip + core * own : b * chip + (core + 1) * own, :] = turned[b * own : (b + 1) * own]
         narrow = taps.astype(BF16)
-        total = jnp.zeros((every, 3 * chip), F32)
         for a in range(3):
-            goal = (2 - a) * chip + core_of * own + inside
-            place = jnp.logical_and(fold[1] == goal, inside < own).astype(F32).astype(BF16)
-            total += jnp.dot(narrow[a * every : (a + 1) * every], place, preferred_element_type=F32)
-        total = total.astype(BF16)
-        for part in range(2):
-            base = pl.multiple_of(b * every + chip * jnp.where(l == part, 0, 1), 16)
-            wb[pl.ds(base, chip), :] = total[part * chip : (part + 1) * chip]
+            for b in range(3):
+                goal = (2 - a) * chip + core * own
+                for part in range(2):
+                    base = pl.multiple_of(b * every + chip * jnp.where(l == part, 0, 1), 16)
+                    start = a * every + part * chip
+                    wb[pl.ds(base, chip), goal : goal + own] = narrow[
+                        start : start + chip, b * own : (b + 1) * own
+                    ]
 
     load_x.wait()
     load_g.wait()
@@ -271,6 +284,9 @@
             remote(pb.at[0, at], arrived.at[to], csend.at[0, k], crecv.at[c, k], chan=other),
             remote(pb.at[1, at], arrived.at[to], csend.at[1, k], crecv.at[c, k], chan=other + 1),
         )
+
+    def chunk_at(s):
+        return jnp.where(s < 2, jnp.where(s == c, chunks - 1, 0), s - 1)
 
     def three(ref, start):
         block = ref[pl.ds(start, 3)]
@@ -296,11 +312,13 @@
                 to = slice((2 * pair + u) * width, (2 * pair + u + 1) * width)
                 for core in range(2):
                     for b in range(3):
-                        s3[core * lanes + b * own : core * lanes + (b + 1) * own, to] = turned[b][
+                        s3[k, core * lanes + b * own : core * lanes + (b + 1) * own, to] = turned[b][
                             core * own : (core + 1) * own
                         ]
+
+    def kernel_terms(k):
         left = jnp.concatenate([three(xs, k * ROWS + u) for u in range(ROWS)], axis=1)
-        term = lax.dot_general(left, s3[...], (((1,), (1,)), ((), ())), preferred_element_type=F32)
+        term = lax.dot_general(left, s3[k], (((1,), (1,)), ((), ())), preferred_element_type=F32)
         for core in range(2):
             acc[core] += term[:, core * lanes : (core + 1) * lanes]
 
@@ -348,10 +366,20 @@
 
         @pl.when(s < chunks)
         def _():
-            k = jnp.where(s < 2, jnp.where(s == c, chunks - 1, 0), s - 1)
+            k = chunk_at(s)
             forward(k)
             for copy in act_copies(k):
                 copy.start()
+
+        @pl.when(jnp.logical_and(s > chunks // 2, s < chunks))
+        def _():
+            kernel_terms(chunk_at(2 * (s - chunks // 2) - 2))
+            kernel_terms(chunk_at(2 * (s - chunks // 2) - 1))
+
+        @pl.when(s == chunks - 1)
+        def _():
+            for t in range(2 * (chunks - 1 - chunks // 2), chunks):
+                kernel_terms(chunk_at(t))
 
         @pl.when(jnp.logical_and(s == c, place < 3))
         def _():
@@ -485,18 +513,17 @@
     chunks = rows // ROWS
     chip, every = 2 * own, 4 * own
     pad_share = round_up(3 * share, 16)
-    pad_own = round_up(own, 128)
     lanes = round_up(3 * own, 128)
     dma = pltpu.SemaphoreType.DMA
     scratch = [
         pltpu.VMEM((rows + 2, every, width), BF16),
         pltpu.VMEM((rows, chip, width), BF16),
         pltpu.VMEM((rows + 2, chip, width), BF16),
-        pltpu.VMEM((2 * lanes, ROWS * width), BF16),
+        pltpu.VMEM((chunks, 2 * lanes, ROWS * width), BF16),
         pltpu.VMEM((2, 3 * every, lanes), F32),
         pltpu.VMEM(kernel.shape, BF16),
-        pltpu.VMEM((3, pad_share, pad_own), F32),
-        pltpu.VMEM((2, side, side, 3, pad_share, pad_own), BF16),
+        pltpu.VMEM((pad_share, lanes), F32),
+        pltpu.VMEM((2, side, side, pad_share, lanes), BF16),
         pltpu.VMEM((3 * every, side * side * pad_share), BF16),
         pltpu.VMEM((3 * chip, 3 * every), BF16),
         pltpu.VMEM((3 * every, 3 * chip), BF16),
@@ -521,6 +548,8 @@
         dma((chunks,)), dma((chunks,)), dma((chunks,)),
         dma((2, chunks)), dma((2, chunks)),
         dma((4, side)), dma((4, side)),
+        dma((side,)), dma((side,)),
+        pltpu.SemaphoreType.REGULAR, pltpu.SemaphoreType.REGULAR,
     ]
     hbm = pl.BlockSpec(memory_space=pl.ANY)
     vmem = pl.BlockSpec(memory_space=pltpu.VMEM)

time: 70.2 us -> 68.4 us (0.974)
  Pallas kernels: 69.5 us -> 67.5 us
    pallas_call x1, Pallas kernels: 67.5 us -> 65.5 us  [shards(): pl.pallas_call(functools.partial(body, side, own, share, height, width),...]
where the time goes in v3:
time: 68.4 us; the launch traced here: 68.2 us
  Pallas kernels  67.5 us (99%)
    pallas_call x1, Pallas kernels, shards(): pl.pallas_call(functools.partial(body, side, own, share, height, width),...  65.5 us
    pallas_call x1, Pallas kernels, shards(): pl.pallas_call(functools.partial(finish, own, share), out_shape=(jax.Shap...  2.02 us

profile of v3, /device:TPU:1, one launch (start us, length us, event | category | flops | bytes accessed | tf_op | source)
XLA Modules:
  0.0 68.2 jit_solution(8754856585033530419)
XLA Ops:
  0.6 65.5 %conv_block.1 = (bf16[64,80,128]{2,1,0:T(8,128)(2,1)S(1)}, f32[64,80,128]{2,1,0:T(8,128)S(1)}, f32[64,256]{1,0:T(8,128)S(1)}) custom-call(bf16[64,80,128]{2,1,0:T(8,128)(2,1)} %bitcast.4, bf16[9,20,80]{2,1,0:T(8,128)(2,1)} %ker.1, bf16[64,80,128]{2,1,0:T(8,128)(2,1)} %bitcast.5), custom_call_target="tpu_custom_call" | custom-call | tf_op jit(solution)/shard_map/conv_block/pallas_call | solution.py:556
  66.1 2.0 %results.1 = (bf16[64,80,128]{2,1,0:T(8,128)(2,1)}, f32[64,80,128]{2,1,0:T(8,128)}, f32[9,20,80]{2,1,0:T(8,128)}) custom-call(bf16[64,80,128]{2,1,0:T(8,128)(2,1)S(1)} %get-tuple-element.9.act, f32[64,80,128]{2,1,0:T(8,128)S(1)} %get-tuple-element.10.grad, f32[64,256]{1,0:T(8,128)S(1)} %get-tuple-element.11.terms), custom_call_target="tpu_custom_call" | custom-call | tf_op jit(solution)/shard_map/results/pallas_call | solution.py:571

commit v4 on v3

--- a/solution.py
+++ b/solution.py
@@ -13,6 +13,7 @@
 F32 = jnp.float32
 ROWS = 4
 PARTS = 4
+LAG = 4
 HELD = 1
 
 
@@ -44,7 +45,7 @@
     arrived, kin, kp, kr, ksum, kr2, kt, kq,
     local, wsend, wrecv, isend, irecv, hsend, hrecv, bsend, brecv,
     ssend, srecv, asend, arecv, alocal, plocal, psend, precv, csend, crecv, ksend, krecv,
-    fsend, frecv, near_ready, far_ready,
+    fsend, frecv, near_ready, plane_ready, slab_ready,
 ):
     rows = height // 2
     chunks = rows // ROWS
@@ -76,17 +77,31 @@
         return s, first * step_first + s * step_second
 
     barrier = pltpu.get_barrier_semaphore()
-    pl.semaphore_signal(barrier, inc=1, device_id={"chan": other + 1}, device_id_type=MESH)
+
+    def tell(sem, **where):
+        pl.semaphore_signal(sem, inc=1, device_id=where, device_id_type=MESH)
+
+    tell(barrier, chan=other + 1)
 
     @pl.when(c == 0)
     def _():
-        pl.semaphore_signal(barrier, inc=1, device_id={"chan": sib}, device_id_type=MESH)
-
-    for to in range(2):
-        pl.semaphore_signal(barrier, inc=1, device_id={"row": 1 - row, "chan": 2 * to}, device_id_type=MESH)
+        tell(barrier, chan=sib)
+
     for k in range(1, side):
         for to in (on_first(k)[1], on_second(k)[1]):
-            pl.semaphore_signal(barrier, inc=1, device_id={"dp": to, "chan": 2 * l}, device_id_type=MESH)
+            tell(barrier, dp=to, chan=0)
+    tell(barrier, row=1 - row, chan=2)
+
+    def agree(teller, number, sem):
+        @pl.when(chan == teller)
+        def _():
+            pl.semaphore_wait(barrier, number)
+            for k in range(1, 4):
+                tell(sem, chan=(teller + k) % 4)
+
+        @pl.when(chan != teller)
+        def _():
+            pl.semaphore_wait(sem, 1)
 
     def mine(ref, first_row, n, g):
         return ref.at[pl.ds(first_row, n), pl.ds(pl.multiple_of(own * g, 16), own)]
@@ -103,7 +118,7 @@
     @pl.when(c == 1)
     def _():
         pl.semaphore_wait(barrier, 3)
-        pl.semaphore_signal(near_ready, inc=1, device_id={"chan": sib}, device_id_type=MESH)
+        tell(near_ready, chan=sib)
 
     @pl.when(c == 0)
     def _():
@@ -145,14 +160,7 @@
             wpk[a * share : (a + 1) * share, b * own : (b + 1) * own] = wk[3 * a + b].astype(F32)
     wraw[c, second, first] = wpk[...].astype(BF16)
 
-    @pl.when(c == 0)
-    def _():
-        pl.semaphore_wait(barrier, 4 + 4 * (side - 1))
-        pl.semaphore_signal(far_ready, inc=1, device_id={"chan": sib}, device_id_type=MESH)
-
-    @pl.when(c == 1)
-    def _():
-        pl.semaphore_wait(far_ready, 1)
+    agree(0, 8 * (side - 1), plane_ready)
 
     gather = []
     for k in range(1, side):
@@ -160,15 +168,6 @@
         copy = remote(spot, spot, wsend.at[0, k], wrecv.at[0, k], dp=on_first(k)[1])
         copy.start()
         gather.append(copy)
-
-    for to in range(2):
-        send(
-            img.at[pl.ds((height - 1) * (1 - row), 1)], mine(xs, (rows + 1) * row, 1, chan),
-            hsend.at[to], hrecv.at[chan], row=1 - row, chan=2 * to + row,
-        )
-    for s in range(3, chunks):
-        for to in range(2):
-            send_piece(to, s)
 
     for core in range(2):
         s3[:, core * lanes + 3 * own : (core + 1) * lanes, :] = jnp.zeros((chunks, lanes - 3 * own, s3.shape[2]), BF16)
@@ -193,6 +192,16 @@
     target = tap * every + owner * share + within - tap * share
     target = jnp.where(within < 3 * share, target, -1)
     em[...] = (lax.broadcasted_iota(jnp.int32, em.shape, 0) == target).astype(F32).astype(BF16)
+
+    agree(2, 4, slab_ready)
+    for to in range(2):
+        send(
+            img.at[pl.ds((height - 1) * (1 - row), 1)], mine(xs, (rows + 1) * row, 1, chan),
+            hsend.at[to], hrecv.at[chan], row=1 - row, chan=2 * to + row,
+        )
+    for s in range(3, chunks):
+        for to in range(2):
+            send_piece(to, s)
 
     for copy in gather:
         copy.wait()
@@ -338,7 +347,9 @@
                     pf[core, q + u] = grad[core * own : (core + 1) * own]
                     pb[core, q + u] = grad[chip + core * own : chip + (core + 1) * own].astype(BF16)
 
-    @pl.loop(0, chunks + 3)
+    steps = chunks + LAG
+
+    @pl.loop(0, steps)
     def _(s):
         @pl.when(s < 2)
         def _():
@@ -371,44 +382,42 @@
             for copy in act_copies(k):
                 copy.start()
 
-        @pl.when(jnp.logical_and(s > chunks // 2, s < chunks))
-        def _():
-            kernel_terms(chunk_at(2 * (s - chunks // 2) - 2))
-            kernel_terms(chunk_at(2 * (s - chunks // 2) - 1))
+        @pl.when(jnp.logical_and(s >= chunks // 2, s < chunks))
+        def _():
+            kernel_terms(chunk_at(2 * s - chunks + 1))
+
+        @pl.when(jnp.logical_and(s >= chunks // 2 - 1, s < chunks - 1))
+        def _():
+            kernel_terms(chunk_at(2 * s - chunks + 2))
+
+        @pl.when(jnp.logical_and(s == c, place < 3))
+        def _():
+            down_copy().start()
+
+        @pl.when(jnp.logical_and(s == 1 - c, place > 0))
+        def _():
+            up_copy().start()
 
         @pl.when(s == chunks - 1)
         def _():
-            for t in range(2 * (chunks - 1 - chunks // 2), chunks):
-                kernel_terms(chunk_at(t))
-
-        @pl.when(jnp.logical_and(s == c, place < 3))
-        def _():
-            down_copy().start()
-
-        @pl.when(jnp.logical_and(s == 1 - c, place > 0))
-        def _():
-            up_copy().start()
-
-        @pl.when(s == chunks - 1)
-        def _():
             trade().start()
 
-        @pl.when(jnp.logical_and(s == chunks + 1, place < 3))
+        @pl.when(jnp.logical_and(s == steps - 2, place < 3))
         def _():
             up_copy().wait_recv()
 
-        @pl.when(jnp.logical_and(s == chunks + 2, place > 0))
+        @pl.when(jnp.logical_and(s == steps - 1, place > 0))
         def _():
             down_copy().wait_recv()
 
-        @pl.when(s >= 3)
-        def _():
-            k = lax.rem(s - 2, chunks)
+        @pl.when(s >= LAG)
+        def _():
+            k = lax.rem(s - LAG + 1, chunks)
             backward(k)
             for copy in near_copies(k):
                 copy.start()
 
-            @pl.when(s < chunks + 3 - HELD)
+            @pl.when(s < steps - HELD)
             def _():
                 for copy in far_copies(k):
                     copy.start()
@@ -446,14 +455,14 @@
     total = ksum[second]
     for k in range(1, side):
         total += kr2[k]
-    kt[...] = total
+    kt[...] = total.astype(BF16)
     copy = remote(kt, kq, ksend.at[3, 0], krecv.at[3, 0], row=1 - row)
     copy.start()
-    for s in range(chunks + 3 - HELD, chunks + 3):
-        for far in far_copies((s - 2) % chunks):
+    for s in range(steps - HELD, steps):
+        for far in far_copies((s - LAG + 1) % chunks):
             far.start()
     copy.wait()
-    kg_out[...] = kt[...] + kq[...]
+    kg_out[...] = kt[...].astype(F32) + kq[...].astype(F32)
 
     @pl.loop(1, chunks + 1)
     def _(k):
@@ -536,8 +545,8 @@
         pltpu.VMEM((side, side, pad_share, lanes), F32),
         pltpu.VMEM((side, pad_share, lanes), F32),
         pltpu.VMEM((side, pad_share, lanes), F32),
-        pltpu.VMEM((pad_share, lanes), F32),
-        pltpu.VMEM((pad_share, lanes), F32),
+        pltpu.VMEM((pad_share, lanes), BF16),
+        pltpu.VMEM((pad_share, lanes), BF16),
         dma((3,)),
         dma((2, side)), dma((2, side)),
         dma((2, chunks)), dma((2, chunks)),
@@ -549,7 +558,7 @@
         dma((2, chunks)), dma((2, chunks)),
         dma((4, side)), dma((4, side)),
         dma((side,)), dma((side,)),
-        pltpu.SemaphoreType.REGULAR, pltpu.SemaphoreType.REGULAR,
+        pltpu.SemaphoreType.REGULAR, pltpu.SemaphoreType.REGULAR, pltpu.SemaphoreType.REGULAR,
     ]
     hbm = pl.BlockSpec(memory_space=pl.ANY)
     vmem = pl.BlockSpec(memory_space=pltpu.VMEM)

time: 68.4 us -> 67.2 us (0.982)
  Pallas kernels: 67.5 us -> 66.4 us
    pallas_call x1, Pallas kernels: 65.5 us -> 64.3 us  [shards(): pl.pallas_call(functools.partial(body, side, own, share, height, width),...]
where the time goes in v4:
time: 67.2 us; the launch traced here: 67 us
  Pallas kernels  66.4 us (99%)
    pallas_call x1, Pallas kernels, shards(): pl.pallas_call(functools.partial(body, side, own, share, height, width),...  64.3 us
    pallas_call x1, Pallas kernels, shards(): pl.pallas_call(functools.partial(finish, own, share), out_shape=(jax.Shap...  2.02 us

profile of v4, /device:TPU:1, one launch (start us, length us, event | category | flops | bytes accessed | tf_op | source)
XLA Modules:
  0.0 67.0 jit_solution(10320647697815140225)
XLA Ops:
  0.6 64.3 %conv_block.1 = (bf16[64,80,128]{2,1,0:T(8,128)(2,1)S(1)}, f32[64,80,128]{2,1,0:T(8,128)S(1)}, f32[64,256]{1,0:T(8,128)S(1)}) custom-call(bf16[64,80,128]{2,1,0:T(8,128)(2,1)} %bitcast.4, bf16[9,20,80]{2,1,0:T(8,128)(2,1)} %ker.1, bf16[64,80,128]{2,1,0:T(8,128)(2,1)} %bitcast.5), custom_call_target="tpu_custom_call" | custom-call | tf_op jit(solution)/shard_map/conv_block/pallas_call | solution.py:565
  65.0 2.0 %results.1 = (bf16[64,80,128]{2,1,0:T(8,128)(2,1)}, f32[64,80,128]{2,1,0:T(8,128)}, f32[9,20,80]{2,1,0:T(8,128)}) custom-call(bf16[64,80,128]{2,1,0:T(8,128)(2,1)S(1)} %get-tuple-element.9.act, f32[64,80,128]{2,1,0:T(8,128)S(1)} %get-tuple-element.10.grad, f32[64,256]{1,0:T(8,128)S(1)} %get-tuple-element.11.terms), custom_call_target="tpu_custom_call" | custom-call | tf_op jit(solution)/shard_map/results/pallas_call | solution.py:580

commit v5 on v4

--- a/solution.py
+++ b/solution.py
@@ -461,38 +461,40 @@
     for s in range(steps - HELD, steps):
         for far in far_copies((s - LAG + 1) % chunks):
             far.start()
-    copy.wait()
-    kg_out[...] = kt[...].astype(F32) + kq[...].astype(F32)
+
+    for old in sent:
+        old.wait_send()
+    border().wait_send()
+
+    @pl.when(place < 3)
+    def _():
+        down_copy().wait_send()
+
+    @pl.when(place > 0)
+    def _():
+        up_copy().wait_send()
+
+    @pl.loop(0, chunks)
+    def _(k):
+        for old in act_copies(k):
+            old.wait()
+
 
     @pl.loop(1, chunks + 1)
     def _(k):
         k = lax.rem(k, chunks)
-        for copy in near_copies(k):
-            copy.wait()
+        for old in near_copies(k):
+            old.wait()
         for of in range(2):
             at = pl.ds(rows * of + k * ROWS, ROWS)
             ref = arrived.at[at]
             remote(ref, ref, csend.at[of, k], crecv.at[of, k], chan=other + of).wait_recv()
             grad_out[at] += arrived[at].astype(F32)
-
-    for copy in sent:
-        copy.wait_send()
-    border().wait_send()
-
-    @pl.when(place < 3)
-    def _():
-        down_copy().wait_send()
-
-    @pl.when(place > 0)
-    def _():
-        up_copy().wait_send()
-
-    @pl.loop(0, chunks)
-    def _(k):
-        for copy in act_copies(k):
-            copy.wait()
-        for copy in far_copies(k):
-            copy.wait_send()
+        for old in far_copies(k):
+            old.wait_send()
+
+    copy.wait()
+    kg_out[...] = kt[...].astype(F32) + kq[...].astype(F32)
 
 
 def finish(own, share, act, grad, terms, act_out, grad_out, kg_out, kg, sems):

time: 67.2 us -> 67 us (level)
  no operation moved by 1% of the time
where the time goes in v5:
time: 67 us; the launch traced here: 66.9 us
  Pallas kernels  66.3 us (99%)
    pallas_call x1, Pallas kernels, shards(): pl.pallas_call(functools.partial(body, side, own, share, height, width),...  64.2 us
    pallas_call x1, Pallas kernels, shards(): pl.pallas_call(functools.partial(finish, own, share), out_shape=(jax.Shap...  2.02 us

profile of v5, /device:TPU:1, one launch (start us, length us, event | category | flops | bytes accessed | tf_op | source)
XLA Modules:
  0.0 66.9 jit_solution(14768512654902695690)
XLA Ops:
  0.6 64.2 %conv_block.1 = (bf16[64,80,128]{2,1,0:T(8,128)(2,1)S(1)}, f32[64,80,128]{2,1,0:T(8,128)S(1)}, f32[64,256]{1,0:T(8,128)S(1)}) custom-call(bf16[64,80,128]{2,1,0:T(8,128)(2,1)} %bitcast.4, bf16[9,20,80]{2,1,0:T(8,128)(2,1)} %ker.1, bf16[64,80,128]{2,1,0:T(8,128)(2,1)} %bitcast.5), custom_call_target="tpu_custom_call" | custom-call | tf_op jit(solution)/shard_map/conv_block/pallas_call | solution.py:567
  64.9 2.0 %results.1 = (bf16[64,80,128]{2,1,0:T(8,128)(2,1)}, f32[64,80,128]{2,1,0:T(8,128)}, f32[9,20,80]{2,1,0:T(8,128)}) custom-call(bf16[64,80,128]{2,1,0:T(8,128)(2,1)S(1)} %get-tuple-element.9.act, f32[64,80,128]{2,1,0:T(8,128)S(1)} %get-tuple-element.10.grad, f32[64,256]{1,0:T(8,128)S(1)} %get-tuple-element.11.terms), custom_call_target="tpu_custom_call" | custom-call | tf_op jit(solution)/shard_map/results/pallas_call | solution.py:582

commit v6 on v5

--- a/solution.py
+++ b/solution.py
@@ -13,7 +13,7 @@
 F32 = jnp.float32
 ROWS = 4
 PARTS = 4
-LAG = 4
+LAG = 3
 HELD = 1
 
 
@@ -150,9 +150,6 @@
     send(cot.at[pl.ds(rows * (1 - c), rows)], mine(gs, 0, rows, c), bsend.at[1], brecv.at[1], chan=sib)
     send_piece(0, 1)
     send_piece(1, 0)
-    for to in range(2):
-        send_piece(to, 2)
-
     wpk[...] = jnp.zeros_like(wpk)
     load_k.wait()
     for b in range(3):
@@ -199,7 +196,7 @@
             img.at[pl.ds((height - 1) * (1 - row), 1)], mine(xs, (rows + 1) * row, 1, chan),
             hsend.at[to], hrecv.at[chan], row=1 - row, chan=2 * to + row,
         )
-    for s in range(3, chunks):
+    for s in range(2, chunks):
         for to in range(2):
             send_piece(to, s)
 

time: 67 us -> 67 us (level)
  no operation moved by 1% of the time
where the time goes in v6:
time: 67 us; the launch traced here: 66.9 us
  Pallas kernels  66.3 us (99%)
    pallas_call x1, Pallas kernels, shards(): pl.pallas_call(functools.partial(body, side, own, share, height, width),...  64.2 us
    pallas_call x1, Pallas kernels, shards(): pl.pallas_call(functools.partial(finish, own, share), out_shape=(jax.Shap...  2.02 us

profile of v6, /device:TPU:1, one launch (start us, length us, event | category | flops | bytes accessed | tf_op | source)
XLA Modules:
  0.0 66.9 jit_solution(13517044864146932775)
XLA Ops:
  0.6 64.2 %conv_block.1 = (bf16[64,80,128]{2,1,0:T(8,128)(2,1)S(1)}, f32[64,80,128]{2,1,0:T(8,128)S(1)}, f32[64,256]{1,0:T(8,128)S(1)}) custom-call(bf16[64,80,128]{2,1,0:T(8,128)(2,1)} %bitcast.4, bf16[9,20,80]{2,1,0:T(8,128)(2,1)} %ker.1, bf16[64,80,128]{2,1,0:T(8,128)(2,1)} %bitcast.5), custom_call_target="tpu_custom_call" | custom-call | tf_op jit(solution)/shard_map/conv_block/pallas_call | solution.py:564
  64.9 2.0 %results.1 = (bf16[64,80,128]{2,1,0:T(8,128)(2,1)}, f32[64,80,128]{2,1,0:T(8,128)}, f32[9,20,80]{2,1,0:T(8,128)}) custom-call(bf16[64,80,128]{2,1,0:T(8,128)(2,1)S(1)} %get-tuple-element.9.act, f32[64,80,128]{2,1,0:T(8,128)S(1)} %get-tuple-element.10.grad, f32[64,256]{1,0:T(8,128)S(1)} %get-tuple-element.11.terms), custom_call_target="tpu_custom_call" | custom-call | tf_op jit(solution)/shard_map/results/pallas_call | solution.py:579
